TPU v7x, 32 devices: a whole 2x2x4 slice. The times are simulated.
32 devices in a mesh: ens: 2 (over y), tile: 4 (over z), row: 2 (over x), lev: 2 (over core).
Axes of the slice: x: 2, y: 2, z: 4, core: 2. Of those that a mesh axis runs over, the one named last changes fastest.
Arguments:
- air_state: float32 [72, 128, 256], P('lev', ('ens', 'tile'), 'row'), parts along dimension 1, may hold values from -6 to 6
- air_kappa: float32 [128, 256], P(('ens', 'tile'), 'row'), parts along dimension 0, may hold values from 0.05 to 0.24
- air_exchange: float32 [128, 256], P(('ens', 'tile'), 'row'), parts along dimension 0, may hold values from 0.2 to 1.5
- air_weights: float32 [72], P('lev'), may hold values from 0.02 to 0.2
- air_profile: float32 [72], P('lev'), may hold values from 0.005 to 0.05
- sea_state: float32 [80, 128, 256], P('lev', ('ens', 'tile'), 'row'), parts along dimension 1, may hold values from -6 to 6
- sea_kappa: float32 [128, 256], P(('ens', 'tile'), 'row'), parts along dimension 0, may hold values from 0.05 to 0.24
- sea_exchange: float32 [128, 256], P(('ens', 'tile'), 'row'), parts along dimension 0, may hold values from 0.2 to 1
- sea_mask: int32 [128, 256], P(('ens', 'tile'), 'row'), parts along dimension 0, may hold values 0 or 1
- sea_weights: float32 [80], P('lev'), may hold values from 0.02 to 0.2
- sea_profile: float32 [80], P('lev'), may hold values from 0.005 to 0.05
- air_counts: int32 [16, 8], P(('ens', 'tile', 'row')), parts along dimension 0, may hold values from 1 to 32, as said below
- air_send: int32 [16, 8, 32], P(('ens', 'tile', 'row')), parts along dimension 0, may hold values from 0 to 2047
- air_source: int32 [16, 2048], P(('ens', 'tile', 'row')), parts along dimension 0, may hold values from 0 to 255, as said below
- air_target: int32 [16, 2048], P(('ens', 'tile', 'row')), parts along dimension 0, may hold values from 0 to 2047
- air_share: float32 [16, 2048], P(('ens', 'tile', 'row')), parts along dimension 0, may hold values from 0.25 to 1
- sea_counts: int32 [16, 8], P(('ens', 'tile', 'row')), parts along dimension 0, may hold values from 1 to 32, as said below
- sea_send: int32 [16, 8, 32], P(('ens', 'tile', 'row')), parts along dimension 0, may hold values from 0 to 2047
- sea_source: int32 [16, 2048], P(('ens', 'tile', 'row')), parts along dimension 0, may hold values from 0 to 255, as said below
- sea_target: int32 [16, 2048], P(('ens', 'tile', 'row')), parts along dimension 0, may hold values from 0 to 2047
- sea_share: float32 [16, 2048], P(('ens', 'tile', 'row')), parts along dimension 0, may hold values from 0.25 to 1
Outputs:
- air_final: float32 [72, 128, 256], P('lev', ('ens', 'tile'), 'row'), parts along dimension 1
- sea_final: float32 [80, 128, 256], P('lev', ('ens', 'tile'), 'row'), parts along dimension 1
There are 2 independent parts, one for each index of `ens`. A program takes and returns all parts, laid end to end along the dimension named above; an argument that names none is the same for every part. Nothing has to cross between parts.
Inputs may be any that keep to these rules, and one draw needn't show every extreme that they name: `air_counts`: each sending device has 32 live slots to some receiving device; about a quarter of the receiving devices may get up to 32 from each sender, the others at most about two thirds of that. `air_source`: row p names s * 32 + c with c < air_counts[s, p]: only live slots are read. `sea_counts`: each sending device has 32 live slots to some receiving device; about a quarter of the receiving devices may get up to 32 from each sender, the others at most about two thirds of that. `sea_source`: row p names s * 32 + c with c < sea_counts[s, p]: only live slots are read.
All inputs are finite; a program needn't handle non-finite values. No bound on the sum of `sea_mask` on one device may be relied on, other than what follows from the above.
Results may differ from a plain program's by a relative error of at most 0.0001.
Values sent between devices are 32-bit elements; how exact they have to be, the bound alone decides.
A program may use at most 64 MiB of HBM per device.

v0:
```python
import functools

import jax
import jax.numpy as jnp
from jax import lax
from jax.experimental import pallas as pl
from jax.experimental.pallas import tpu as pltpu
from jax.sharding import PartitionSpec as P

AIR_STEPS = 4
SEA_STEPS = 2
F32 = jnp.float32
DIRS = tuple((dt, dr) for dt in (-1, 0, 1) for dr in (-1, 0, 1) if (dt, dr) != (0, 0))
LANE = 128
FIRST = (0, 5, 3, 9)
SECOND = (1, 2, 4, 6, 7, 8, 10, 11, 12, 13, 14, 15, 16, 17, 18, 19, 20)
PER = 16


def iota(shape, dim):
    return lax.broadcasted_iota(jnp.int32, shape, dim)


def turn(x, shift, axis):
    return pltpu.roll(x, shift % x.shape[axis], axis)


def lap_wrapped(x):
    return (
        turn(x, 1, 0) + turn(x, -1, 0) + turn(x, 1, 1) + turn(x, -1, 1) - 4.0 * x
    )


def repeat_8(x, low):
    y = jnp.where(low, x, 0.0)
    for width in (8, 16, 32, 64):
        y = y + turn(y, width, 1)
    return y


def kernel(n_tile, n_row, *refs):
    operands, (air_out, sea_out) = refs[:21], refs[21:23]
    held, rest = refs[23:44], refs[44:]
    (
        air_ref, ka_ref, ea_ref, aw_ref, ap_ref,
        sea_ref, ko_ref, eo_ref, mask_ref, ow_ref, op_ref,
        acnt_ref, asend_ref, asrc_ref, atgt_ref, ashr_ref,
        ocnt_ref, osend_ref, osrc_ref, otgt_ref, oshr_ref,
    ) = held
    (
        in_sem,
        ext1, ext2, ext3, rows_send, rows_recv, lev_send, lev_recv,
        slot_send, slot_recv, index_ref, onehot_ref, edge_air, edge_sea,
        send1, recv1, send2, recv2, send3, recv3,
        rs_send, rs_recv, lv_send, lv_recv, sl_send, sl_recv,
    ) = rest

    def fetch(i):
        return pltpu.make_async_copy(operands[i], held[i], in_sem.at[i])

    for i in FIRST + SECOND:
        fetch(i).start()

    t = lax.axis_index("tile")
    r = lax.axis_index("row")
    lev = lax.axis_index("lev")
    me = t * n_row + r
    peers = n_tile * n_row
    n_air = air_ref.shape[0]
    n_sea = sea_ref.shape[0]
    g_air = (n_air + PER - 1) // PER
    g_sea = (n_sea + PER - 1) // PER
    planes = g_air + g_sea
    cap = asend_ref.shape[2]
    entries = asrc_ref.shape[1]
    MESH = pl.DeviceIdType.MESH

    barrier = pltpu.get_barrier_semaphore()

    def greet(p, carry):
        @pl.when(p != me)
        def _():
            pl.semaphore_signal(
                barrier, inc=1, device_id={"tile": p // n_row, "row": p % n_row},
                device_id_type=MESH,
            )
        return carry

    lax.fori_loop(0, peers, greet, 0)
    pl.semaphore_signal(barrier, inc=1, device_id={"lev": 1 - lev}, device_id_type=MESH)

    lane16 = iota((16, LANE), 1)
    group16 = lane16 // 8

    def column_sum(state_ref, weights_ref, count):
        totals = [weights_ref[k] * state_ref[k] for k in range(4)]
        for k in range(4, count):
            totals[k % 4] = totals[k % 4] + weights_ref[k] * state_ref[k]
        return (totals[0] + totals[1]) + (totals[2] + totals[3])

    def strips(state_ref, count, base):
        for i in range((count + PER - 1) // PER):
            acc = jnp.zeros((16, LANE), F32)
            for j in range(PER):
                k = i * PER + j
                if k < count:
                    acc = jnp.where(group16 == j, turn(state_ref[k], 8 * j + 4, 1), acc)
            ext1[base + i, 8:24, LANE:2 * LANE] = acc

    def weight_of_flux(weights_ref, profile_ref, count):
        total = weights_ref[0] * profile_ref[0]
        for k in range(1, count):
            total = total + weights_ref[k] * profile_ref[k]
        return total

    lev_copy = pltpu.make_async_remote_copy(
        src_ref=lev_send, dst_ref=lev_recv, send_sem=lv_send, recv_sem=lv_recv,
        device_id={"lev": 1 - lev}, device_id_type=MESH,
    )
    for i in FIRST:
        fetch(i).wait()
    lev_send[0:16, :] = column_sum(air_ref, aw_ref, n_air)
    lev_send[16:32, :] = column_sum(sea_ref, ow_ref, n_sea)
    for i in SECOND:
        fetch(i).wait()
    lev_send[32:40, :] = jnp.zeros((8, LANE), F32) + weight_of_flux(aw_ref, ap_ref, n_air)
    lev_send[40:48, :] = jnp.zeros((8, LANE), F32) + weight_of_flux(ow_ref, op_ref, n_sea)
    pl.semaphore_wait(barrier, peers)
    lev_copy.start()

    strips(air_ref, n_air, 0)
    strips(sea_ref, n_sea, g_air)
    land_sea = mask_ref[...].astype(F32)
    ext1[planes, 8:24, LANE:2 * LANE] = ka_ref[...]
    ext1[planes + 1, 8:24, LANE:2 * LANE] = ea_ref[...]
    ext1[planes + 2, 8:24, LANE:2 * LANE] = land_sea * ko_ref[...]
    ext1[planes + 3, 8:24, LANE:2 * LANE] = land_sea * eo_ref[...]

    sub = iota((8, LANE), 0)
    upper = sub < 4

    def pack_rows(state_ref, count, base):
        for j in range(count // 2):
            a, b = state_ref[2 * j], state_ref[2 * j + 1]
            rows_send[0, base + j] = jnp.where(upper, a[0:8], turn(b[0:8], 4, 0))
            rows_send[1, base + j] = jnp.where(upper, turn(a[8:16], 4, 0), b[8:16])

    def exists(dt, dr):
        ok = jnp.bool_(True)
        if dt < 0:
            ok = ok & (t + dt >= 0)
        if dt > 0:
            ok = ok & (t + dt < n_tile)
        if dr < 0:
            ok = ok & (r + dr >= 0)
        if dr > 0:
            ok = ok & (r + dr < n_row)
        return ok

    def halo_copy(ext, send, recv, d):
        dt, dr = DIRS[d]
        source_rows = {-1: (8, 16), 0: (8, 24), 1: (16, 24)}[dt]
        target_rows = {-1: (24, 32), 0: (8, 24), 1: (0, 8)}[dt]
        target_lanes = {-1: 2 * LANE, 0: LANE, 1: 0}[dr]
        return pltpu.make_async_remote_copy(
            src_ref=ext.at[:, source_rows[0]:source_rows[1], LANE:2 * LANE],
            dst_ref=ext.at[:, target_rows[0]:target_rows[1], target_lanes:target_lanes + LANE],
            send_sem=send.at[d],
            recv_sem=recv.at[d],
            device_id={"tile": t + dt, "row": r + dr},
            device_id_type=MESH,
        )

    def halo_start(ext, send, recv):
        for d, (dt, dr) in enumerate(DIRS):
            @pl.when(exists(dt, dr))
            def _():
                halo_copy(ext, send, recv, d).start()

    def halo_clear(ext):
        for dt, dr in DIRS:
            rows = {-1: (24, 32), 0: (8, 24), 1: (0, 8)}[dt]
            lanes = {-1: 2 * LANE, 0: LANE, 1: 0}[dr]
            @pl.when(jnp.logical_not(exists(-dt, -dr)))
            def _():
                ext[:, rows[0]:rows[1], lanes:lanes + LANE] = jnp.zeros(
                    (ext.shape[0], rows[1] - rows[0], LANE), F32
                )

    def halo_wait_recv(ext, send, recv):
        for d, (dt, dr) in enumerate(DIRS):
            @pl.when(exists(-dt, -dr))
            def _():
                halo_copy(ext, send, recv, d).wait_recv()

    def halo_wait_send(ext, send, recv):
        for d, (dt, dr) in enumerate(DIRS):
            @pl.when(exists(dt, dr))
            def _():
                halo_copy(ext, send, recv, d).wait_send()

    def rows_copy(d):
        return pltpu.make_async_remote_copy(
            src_ref=rows_send.at[d], dst_ref=rows_recv.at[d],
            send_sem=rs_send.at[d], recv_sem=rs_recv.at[d],
            device_id={"tile": t + (1 if d else -1)}, device_id_type=MESH,
        )

    halo_start(ext1, send1, recv1)
    pack_rows(air_ref, n_air, 0)
    pack_rows(sea_ref, n_sea, n_air // 2)
    for d in range(2):
        @pl.when(exists(1 if d else -1, 0))
        def _():
            rows_copy(d).start()

        @pl.when(jnp.logical_not(exists(-1 if d else 1, 0)))
        def _():
            rows_recv[d] = jnp.zeros(rows_recv.shape[1:], F32)
    halo_clear(ext1)
    halo_clear(ext2)
    halo_clear(ext3)

    cells = 16 * LANE
    index_ref[...] = jnp.zeros(index_ref.shape, jnp.int32)
    index_ref[:, 0:cap] = asend_ref[0]
    index_ref[:, cap:2 * cap] = osend_ref[0] + cells
    index = index_ref[...]
    on_diagonal = iota((peers, peers), 0) == iota((peers, peers), 1)

    def live_count(counts_ref):
        counts = jnp.broadcast_to(counts_ref[...].astype(F32), (peers, peers))
        return jnp.sum(jnp.where(on_diagonal, counts, 0.0), axis=1, keepdims=True)

    slot_lane = iota((peers, LANE), 1)
    limit = jnp.where(slot_lane < cap, live_count(acnt_ref), live_count(ocnt_ref))
    limit = jnp.where(slot_lane < 2 * cap, limit, 0.0)
    live = (slot_lane % cap).astype(F32) < limit
    index_lane = index % LANE
    index_row = index // LANE

    lev_copy.wait_recv()
    surface = lev_send[...] + lev_recv[...]
    ext2[0, 8:24, LANE:2 * LANE] = surface[0:16]
    ext2[1, 8:24, LANE:2 * LANE] = surface[16:32]
    values = jnp.zeros((peers, LANE), F32)
    for x in range(32):
        row = jnp.broadcast_to(surface[x:x + 1], (peers, LANE))
        picked = jnp.take_along_axis(row, index_lane, axis=1, mode="promise_in_bounds")
        values = jnp.where(index_row == x, picked, values)
    values = jnp.where(live, values, 0.0)
    slot_send[...] = values.reshape(peers, 1, LANE)

    def slot_copy(p, recv_slot):
        return pltpu.make_async_remote_copy(
            src_ref=slot_send.at[p], dst_ref=slot_recv.at[recv_slot],
            send_sem=sl_send.at[p], recv_sem=sl_recv.at[recv_slot],
            device_id={"tile": p // n_row, "row": p % n_row}, device_id_type=MESH,
        )

    def others(action):
        def step(p, carry):
            @pl.when(p != me)
            def _():
                action(p)
            return carry
        lax.fori_loop(0, peers, step, 0)

    others(lambda p: slot_copy(p, me).start())
    halo_start(ext2, send2, recv2)
    slot_recv[me] = slot_send[me]

    cell_y = iota((LANE, LANE), 0)
    for m, tgt_ref in enumerate((atgt_ref, otgt_ref)):
        for c in range(entries // LANE):
            y = tgt_ref[0:1, c * LANE:(c + 1) * LANE] % LANE
            onehot_ref[m, :, c * LANE:(c + 1) * LANE] = jnp.where(
                jnp.broadcast_to(y, (LANE, LANE)) == cell_y, 1.0, 0.0
            ).astype(jnp.bfloat16)

    others(lambda p: slot_copy(p, p).wait_recv())
    table = slot_recv[...].reshape(peers, LANE)
    cell_x = iota((16, LANE), 0)
    sender = iota((peers, LANE), 0)
    for m, (src_ref, tgt_ref, shr_ref) in enumerate(
        ((asrc_ref, atgt_ref, ashr_ref), (osrc_ref, otgt_ref, oshr_ref))
    ):
        parts = ([], [], [])
        for c in range(entries // LANE):
            at = slice(c * LANE, (c + 1) * LANE)
            source = jnp.broadcast_to(src_ref[0:1, at], (peers, LANE))
            picked = jnp.take_along_axis(
                table, source % cap + m * cap, axis=1, mode="promise_in_bounds"
            )
            value = jnp.sum(jnp.where(source // cap == sender, picked, 0.0), axis=0, keepdims=True)
            value = value * shr_ref[0:1, at]
            x = jnp.broadcast_to(tgt_ref[0:1, at] // LANE, (16, LANE))
            spread = jnp.where(x == cell_x, jnp.broadcast_to(value, (16, LANE)), 0.0)
            high = spread.astype(jnp.bfloat16)
            rest = spread - high.astype(F32)
            middle = rest.astype(jnp.bfloat16)
            low = (rest - middle.astype(F32)).astype(jnp.bfloat16)
            parts[0].append(high)
            parts[1].append(middle)
            parts[2].append(low)
        left = jnp.concatenate([jnp.concatenate(p, axis=1) for p in parts], axis=0)
        product = lax.dot_general(
            left, onehot_ref[m], (((1,), (1,)), ((), ())), preferred_element_type=F32
        )
        ext3[1 - m, 8:24, LANE:2 * LANE] = product[0:16] + product[16:32] + product[32:48]
    halo_start(ext3, send3, recv3)

    halo_wait_recv(ext1, send1, recv1)
    for d in range(2):
        @pl.when(exists(-1 if d else 1, 0))
        def _():
            rows_copy(d).wait_recv()

    lane32 = iota((32, LANE), 1)
    low_lanes = lane32 < 8
    left_half = lane32 % 8 < 4
    lane24 = iota((24, LANE), 1)
    first_lane = lane24 == 0
    last_lane = lane24 == LANE - 1

    def advance(state_ref, out_ref, edge_ref, count, base, rows_base, plane, steps):
        kl = repeat_8(turn(ext1[plane, :, 0:LANE], 4, 1), low_lanes)
        kc = repeat_8(turn(ext1[plane, :, LANE:2 * LANE], 4, 1), low_lanes)
        kr = repeat_8(turn(ext1[plane, :, 2 * LANE:], 4, 1), low_lanes)
        kappa_left = jnp.where(left_half, kl, kc)
        kappa_right = jnp.where(left_half, kc, kr)
        kappa = ext1[plane, 4:28, LANE:2 * LANE]
        for i in range((count + PER - 1) // PER):
            own = ext1[base + i, :, LANE:2 * LANE]
            left = jnp.where(left_half, ext1[base + i, :, 0:LANE], own)
            right = jnp.where(left_half, own, ext1[base + i, :, 2 * LANE:])
            for n in range(steps):
                edge = jnp.where(lane32 % 8 == 3, left, turn(right, -2, 1))
                edge_ref[n, i] = edge[4:28]
                if n + 1 < steps:
                    left = left + kappa_left * lap_wrapped(left)
                    right = right + kappa_right * lap_wrapped(right)

        def group(h, carry):
            fields, places = [], []
            for b in range(levels):
                k = h * levels + b
                q = k // 2
                top, bottom = rows_recv[1, rows_base + q], rows_recv[0, rows_base + q]
                if b % 2:
                    top = turn(top, 4, 0)
                else:
                    bottom = turn(bottom, 4, 0)
                a = turn(state_ref[k, 0:8, :], 4, 0)
                c = turn(state_ref[k, 8:16, :], 4, 0)
                fields.append(jnp.concatenate(
                    [jnp.where(upper, top, a), jnp.where(upper, a, c), jnp.where(upper, c, bottom)],
                    axis=0,
                ))
                places.append((k // PER, (2 * LANE - 3 - 8 * (k % PER)) % LANE))
            for n in range(steps):
                for b in range(levels):
                    x = fields[b]
                    i, shift = places[b]
                    edge = pltpu.roll(edge_ref[n, i], shift, 1)
                    around = (
                        turn(x, 1, 0) + turn(x, -1, 0)
                        + jnp.where(first_lane, edge, turn(x, 1, 1))
                        + jnp.where(last_lane, edge, turn(x, -1, 1))
                    )
                    fields[b] = x + kappa * (around - 4.0 * x)
            for b in range(levels):
                x = fields[b]
                k = h * levels + b
                a, c, e = turn(x[0:8], 4, 0), turn(x[8:16], 4, 0), turn(x[16:24], 4, 0)
                out_ref[k, 0:8, :] = jnp.where(upper, a, c)
                out_ref[k, 8:16, :] = jnp.where(upper, c, e)
            return carry

        levels = max(v for v in (2, 4, 6, 8) if count % v == 0)
        lax.fori_loop(0, count // levels, group, 0)

    advance(air_ref, air_out, edge_air, n_air, 0, 0, planes, AIR_STEPS)
    advance(sea_ref, sea_out, edge_sea, n_sea, g_air, n_air // 2, planes + 2, SEA_STEPS)

    halo_wait_recv(ext2, send2, recv2)
    halo_wait_recv(ext3, send3, recv3)
    for m, (out_ref, profile_ref, count, steps) in enumerate(
        ((air_out, ap_ref, n_air, AIR_STEPS), (sea_out, op_ref, n_sea, SEA_STEPS))
    ):
        flux_weight = surface[32 + 8 * m:33 + 8 * m]
        flux_weight = jnp.concatenate([flux_weight] * 3, axis=1)
        kappa = ext1[planes + 2 * m]
        exchange = ext1[planes + 2 * m + 1]
        s = ext2[m]
        q = ext3[m]
        g = None
        for n in range(steps):
            flux = exchange * (q - s)
            g = flux if g is None else g + kappa * lap_wrapped(g) + flux
            if n + 1 < steps:
                s = s + kappa * lap_wrapped(s) + flux_weight * flux
        center = g[8:24, LANE:2 * LANE]
        for k in range(count):
            out_ref[k] = out_ref[k] + profile_ref[k] * center

    lev_copy.wait_send()
    others(lambda p: slot_copy(p, me).wait_send())
    halo_wait_send(ext1, send1, recv1)
    halo_wait_send(ext2, send2, recv2)
    halo_wait_send(ext3, send3, recv3)
    for d in range(2):
        @pl.when(exists(1 if d else -1, 0))
        def _():
            rows_copy(d).wait_send()


def body(*args):
    air, sea = args[0], args[5]
    n_air, n_sea = air.shape[0], sea.shape[0]
    n_tile, n_row = lax.axis_size("tile"), lax.axis_size("row")
    peers = n_tile * n_row
    entries = args[13].shape[1]
    g_air, g_sea = -(-n_air // PER), -(-n_sea // PER)
    vmem = pl.BlockSpec(memory_space=pltpu.VMEM)
    hbm = pl.BlockSpec(memory_space=pltpu.HBM)
    scalars = (3, 4, 9, 10)
    packed = (n_air + n_sea) // 2
    DMA = pltpu.SemaphoreType.DMA
    return pl.pallas_call(
        functools.partial(kernel, n_tile, n_row),
        out_shape=(
            jax.ShapeDtypeStruct(air.shape, F32),
            jax.ShapeDtypeStruct(sea.shape, F32),
        ),
        in_specs=[hbm] * len(args),
        out_specs=(vmem, vmem),
        scratch_shapes=[
            (pltpu.SMEM if i in scalars else pltpu.VMEM)(v.shape, v.dtype)
            for i, v in enumerate(args)
        ] + [
            DMA((len(args),)),
            pltpu.VMEM((g_air + g_sea + 4, 32, 3 * LANE), F32),
            pltpu.VMEM((2, 32, 3 * LANE), F32),
            pltpu.VMEM((2, 32, 3 * LANE), F32),
            pltpu.VMEM((2, packed, 8, LANE), F32),
            pltpu.VMEM((2, packed, 8, LANE), F32),
            pltpu.VMEM((48, LANE), F32),
            pltpu.VMEM((48, LANE), F32),
            pltpu.VMEM((peers, 1, LANE), F32),
            pltpu.VMEM((peers, 1, LANE), F32),
            pltpu.VMEM((peers, LANE), jnp.int32),
            pltpu.VMEM((2, LANE, entries), jnp.bfloat16),
            pltpu.VMEM((AIR_STEPS, g_air, 24, LANE), F32),
            pltpu.VMEM((SEA_STEPS, g_sea, 24, LANE), F32),
            DMA((8,)), DMA((8,)), DMA((8,)), DMA((8,)), DMA((8,)), DMA((8,)),
            DMA((2,)), DMA((2,)), DMA, DMA, DMA((peers,)), DMA((peers,)),
        ],
        compiler_params=pltpu.CompilerParams(
            collective_id=0, has_side_effects=True, vmem_limit_bytes=60 * 1024 * 1024
        ),
    )(*args)


def solution(mesh):
    field = P("lev", ("ens", "tile"), "row")
    cell = P(("ens", "tile"), "row")
    level = P("lev")
    table = P(("ens", "tile", "row"), None)
    lists = P(("ens", "tile", "row"), None, None)
    placed = (
        field, cell, cell, level, level,
        field, cell, cell, cell, level, level,
        table, lists, table, table, table,
        table, lists, table, table, table,
    )
    return jax.shard_map(
        body, mesh=mesh, in_specs=placed, out_specs=(field, field), check_vma=False
    )
```

profile of v0, /device:TPU:0, one launch (start us, length us, event | category | flops | bytes accessed | tf_op | source)
XLA Modules:
  0.0 24.4 jit_solution(15577357468562348232)
XLA Ops:
  0.6 21.2 %shard_map.212 = (f32[36,16,128]{2,1,0:T(8,128)}, f32[40,16,128]{2,1,0:T(8,128)}) custom-call(f32[36,16,128]{2,1,0:T(8,128)} %refs_0_.1, f32[16,128]{1,0:T(8,128)} %refs_1_.1, f32[16,128]{1,0:T(8,128)} %refs_2_.1, f32[36]{0:T(128)} %refs_3_.1, f32[36]{0:T(128)} %refs_4_.1, f32[40,16,128]{2,1,0:T(8,128)} %refs_5_.1, f32[16,128]{1,0:T(8,128)} %refs_6_.1, ...), custom_call_target="tpu_custom_call" | custom-call | tf_op jit(solution)/shard_map/pallas_call | solution.py:430
  21.9 0.0 copy-start
  21.9 1.7 %copy.25 = f32[36,16,128]{2,1,0:T(8,128)} copy(f32[36,16,128]{2,1,0:T(8,128)} %get-tuple-element.4) | data formatting | bytes 589824
  23.6 0.0 copy-done
  23.6 0.7 %copy.26 = f32[40,16,128]{2,1,0:T(8,128)} copy(f32[40,16,128]{2,1,0:T(8,128)S(1)} %copy-done) | data formatting | bytes 655360
Async XLA Ops:
  21.9 1.8 %copy-start = (f32[40,16,128]{2,1,0:T(8,128)S(1)}, f32[40,16,128]{2,1,0:T(8,128)}, u32[]{:S(2)}) copy-start(f32[40,16,128]{2,1,0:T(8,128)} %get-tuple-element.5) | copy-start | bytes 983044
where the time goes:
time: 24.5 us; the launch traced here: 24.4 us
  Pallas kernels  21.2 us (87%)
  local copies, waits for them, and re-layouts  2.47 us (10%)
  between operations  0.66 us (3%)
    pallas_call x1, Pallas kernels, body(): pl.pallas_call(functools.partial(kernel, n_tile, n_row), out_shape=(jax.S...  21.2 us
    unnamed x4, local copies, waits for them, and re-layouts  2.47 us

commit v1 on v0

--- a/solution.py
+++ b/solution.py
@@ -121,12 +121,15 @@
         fetch(i).wait()
     lev_send[0:16, :] = column_sum(air_ref, aw_ref, n_air)
     lev_send[16:32, :] = column_sum(sea_ref, ow_ref, n_sea)
-    for i in SECOND:
+    for i in (4, 10):
         fetch(i).wait()
     lev_send[32:40, :] = jnp.zeros((8, LANE), F32) + weight_of_flux(aw_ref, ap_ref, n_air)
     lev_send[40:48, :] = jnp.zeros((8, LANE), F32) + weight_of_flux(ow_ref, op_ref, n_sea)
     pl.semaphore_wait(barrier, peers)
     lev_copy.start()
+    for i in SECOND:
+        if i not in (4, 10):
+            fetch(i).wait()
 
     strips(air_ref, n_air, 0)
     strips(sea_ref, n_sea, g_air)

time: 24.5 us -> 24.5 us (level)
  no operation moved by 1% of the time
where the time goes in v1:
time: 24.5 us; the launch traced here: 24.4 us
  Pallas kernels  21.2 us (87%)
  local copies, waits for them, and re-layouts  2.47 us (10%)
  between operations  0.66 us (3%)
    pallas_call x1, Pallas kernels, body(): pl.pallas_call(functools.partial(kernel, n_tile, n_row), out_shape=(jax.S...  21.2 us
    unnamed x4, local copies, waits for them, and re-layouts  2.47 us

profile of v1, /device:TPU:0, one launch (start us, length us, event | category | flops | bytes accessed | tf_op | source)
XLA Modules:
  0.0 24.4 jit_solution(15395781952961766330)
XLA Ops:
  0.6 21.2 %shard_map.212 = (f32[36,16,128]{2,1,0:T(8,128)}, f32[40,16,128]{2,1,0:T(8,128)}) custom-call(f32[36,16,128]{2,1,0:T(8,128)} %refs_0_.1, f32[16,128]{1,0:T(8,128)} %refs_1_.1, f32[16,128]{1,0:T(8,128)} %refs_2_.1, f32[36]{0:T(128)} %refs_3_.1, f32[36]{0:T(128)} %refs_4_.1, f32[40,16,128]{2,1,0:T(8,128)} %refs_5_.1, f32[16,128]{1,0:T(8,128)} %refs_6_.1, ...), custom_call_target="tpu_custom_call" | custom-call | tf_op jit(solution)/shard_map/pallas_call | solution.py:433
  21.9 0.0 copy-start
  21.9 1.7 %copy.25 = f32[36,16,128]{2,1,0:T(8,128)} copy(f32[36,16,128]{2,1,0:T(8,128)} %get-tuple-element.4) | data formatting | bytes 589824
  23.6 0.0 copy-done
  23.6 0.7 %copy.26 = f32[40,16,128]{2,1,0:T(8,128)} copy(f32[40,16,128]{2,1,0:T(8,128)S(1)} %copy-done) | data formatting | bytes 655360
Async XLA Ops:
  21.9 1.8 %copy-start = (f32[40,16,128]{2,1,0:T(8,128)S(1)}, f32[40,16,128]{2,1,0:T(8,128)}, u32[]{:S(2)}) copy-start(f32[40,16,128]{2,1,0:T(8,128)} %get-tuple-element.5) | copy-start | bytes 983044
